TPU v7x, 512 devices: a whole 4x8x8 slice. The times are simulated.
512 devices in a mesh: sub: 64 (over z, y), grp: 8 (over x, core).
Axes of the slice: x: 4, y: 8, z: 8, core: 2. Of those that a mesh axis runs over, the one named last changes fastest.
Arguments:
- vectors: bfloat16 [8, 64, 1024, 512], P('grp', 'sub'), may hold values from -6 to 6
- blocks: bfloat16 [8, 64, 1024, 1024], P('grp', 'sub'), may hold values from -0.1875 to 0.1875
- basis: bfloat16 [8, 64, 1024, 128], P('grp', 'sub'), may hold values from -0.25 to 0.25
- transfer: bfloat16 [8, 64, 9, 128, 128], P('grp', 'sub'), as said below
- coupling: bfloat16 [8, 64, 9, 128, 128], P('grp', 'sub'), as said below
Outputs:
- applied: bfloat16 [8, 64, 1024, 512], P('grp', 'sub')
Inputs may be any that keep to these rules, and one draw needn't show every extreme that they name: transfer[g, s, l] is the same for all leaves g * 64 + s of one level-l node. coupling[g, s, l] is the same for all leaves g * 64 + s of one level-l node.
All inputs are finite; a program needn't handle non-finite values.
Results may differ from a plain program's by a relative error of at most 0.0047.
Values may be sent and summed in bfloat16 or wider, within the bound.
A program may use at most 64 MiB of HBM per device.

v0:
```python
import functools

import jax
import jax.numpy as jnp
from jax import lax
from jax.experimental import pallas as pl
from jax.experimental.pallas import tpu as pltpu
from jax.sharding import PartitionSpec as P

MESH = pl.DeviceIdType.MESH
BF = jnp.bfloat16
F32 = jnp.float32


def dot(left, right):
    return jnp.dot(left, right, preferred_element_type=F32)


def dot_nt(left, right):
    return lax.dot_general(left, right, (((1,), (1,)), ((), ())), preferred_element_type=F32)


def dot_tn(left, right):
    return lax.dot_general(left, right, (((0,), (0,)), ((), ())), preferred_element_type=F32)


def split(value):
    high = value.astype(BF)
    return high, (value - high.astype(F32)).astype(BF)


def flip(index, offset):
    out = index
    for bit in range(offset.bit_length()):
        if offset >> bit & 1:
            out = out + (1 << bit) - (2 << bit) * lax.rem(lax.div(index, 1 << bit), 2)
    return out


def level_of(offset):
    return offset.bit_length() - 1


def far_first(count):
    return [j for j in (4, 5, 3, 7, 6, 2, 1) if j < count]


def wait_bytes(ref, sem):
    pltpu.make_async_copy(ref, ref, sem).wait()


def up_weight(product):
    high, low = split(product)
    return jnp.concatenate([high, high, low], axis=0)


def up_exact(matrix):
    return jnp.concatenate([matrix, matrix, jnp.zeros_like(matrix)], axis=0)


def wide(value):
    high, low = split(value)
    return jnp.concatenate([high, low, high], axis=1)


def times_exact(product, matrix):
    high, low = split(product)
    return dot(high, matrix) + dot(low, matrix)


def kernel(dims, x_hbm, d_hbm, u_hbm, t_hbm, b_hbm, near, lift_out, far_out,
           xv, dv, uv, ut, tv, bv,
           rt, bt, wy, wx, wzl, vx, vz, vw, vg,
           h_send, h_recv, cy_send, cy_recv, cl_send, cl_recv,
           cz_send, cz_recv, zs_send, zs_recv, x_send, x_recv,
           far_y_send, far_y,
           load_sem, send_sem, recv_sem):
    lz, lx = dims
    ly = 3
    ny, nz, nx = 1 << ly, 1 << lz, 1 << lx
    leaf, vecs = x_hbm.shape
    rank = u_hbm.shape[1]
    yblk = vecs // ny
    sub, grp = lax.axis_index("sub"), lax.axis_index("grp")
    y, z = lax.rem(sub, ny), lax.div(sub, ny)

    def y_peer(j):
        return {"sub": z * ny + flip(y, j)}

    def z_peer(j):
        return {"sub": flip(z, j) * ny + y}

    def x_peer(j):
        return {"grp": flip(grp, j)}

    def rows(index, size):
        return pl.ds(pl.multiple_of(index * size, size), size)

    def send(src, dst, group, peer):
        pltpu.make_async_remote_copy(
            src_ref=src, dst_ref=dst, send_sem=send_sem.at[group], recv_sem=recv_sem.at[group],
            device_id=peer, device_id_type=MESH,
        ).start()

    barrier = pltpu.get_barrier_semaphore()
    peers = []
    for j in far_first(8):
        peers += [peer(j) for peer, count in ((y_peer, ny), (z_peer, nz), (x_peer, nx)) if j < count]
    for peer in peers:
        pl.semaphore_signal(barrier, inc=1, device_id=peer, device_id_type=MESH)

    head = leaf // 2
    loads = {}
    for i, (name, src, dst) in enumerate((
        ("u", u_hbm, uv),
        ("x0", x_hbm.at[pl.ds(0, head)], xv.at[pl.ds(0, head)]),
        ("x1", x_hbm.at[pl.ds(head, head)], xv.at[pl.ds(head, head)]),
        ("t", t_hbm, tv),
        ("d", d_hbm, dv),
        ("b", b_hbm, bv),
    )):
        loads[name] = pltpu.make_async_copy(src, dst, load_sem.at[i])
        loads[name].start()

    pair = lax.div(y, 2)
    outward = 2 * lax.rem(y, 2) - 1

    def spread(src, dst, group):
        for k in (3, 2, 1):
            target = lax.rem(y + k * outward + ny, ny)
            other = lax.div(target, 2)
            slot = lax.rem(pair + other, 2) + 2 * lax.rem(lax.div(pair, 2) + lax.div(other, 2), 2)
            send(src.at[1], dst.at[slot], group, {"sub": z * ny + target})
        send(src.at[2], dst.at[4], group, y_peer(6))

    def climb(base, levels):
        product = tv[base].astype(F32)
        chain = [product]
        for level in range(1, levels):
            product = times_exact(product, tv[base + level])
            chain.append(product)
        return chain

    def down(products, base, levels):
        parts = [bv[base].T]
        for i in range(1, levels):
            parts.append(up_weight(times_exact(products[i - 1], bv[base + i]).T))
        return jnp.concatenate(parts, axis=0)

    def near_part(part, parts):
        size = vecs // parts
        at = pl.ds(part * size, size)
        near[:, at] = dot(dv[...], xv[:, at])

    loads["t"].wait()
    ty = climb(0, ly)
    wy[...] = up_weight(ty[ly - 1])
    loads["u"].wait()
    ut[...] = uv[...].T
    loads["x0"].wait()
    hat_t = dot(ut[:, :head], xv[:head, :])
    loads["x1"].wait()
    hat = (hat_t + dot(ut[:, head:], xv[head:, :])).T
    hat_w = wide(hat)
    cy_send[...] = dot(hat_w, wy[...]).astype(BF)
    pl.semaphore_wait(barrier, len(peers))
    for j in far_first(ny):
        send(cy_send.at[rows(flip(y, j), yblk)], cy_recv.at[j], 0, y_peer(j))

    cl_send[...] = dot(hat_w[:, :2 * rank], jnp.concatenate([tv[0], tv[0]], axis=0)).astype(BF)
    h_send[...] = hat.astype(BF)
    tz = climb(ly, lz + lx - 1)
    wx[...] = jnp.concatenate([up_weight(product) for product in tz[lz - 1:]], axis=1)
    if lz > 1:
        wzl[...] = jnp.concatenate([up_exact(tv[ly])] + [up_weight(tz[i]) for i in range(1, lz - 1)], axis=1)
    lift_out[...] = jnp.concatenate(split(dot(uv[...], tv[0])), axis=1)
    loads["d"].wait()
    near_part(0, 2)
    for j in far_first(ny):
        send(cl_send.at[rows(flip(y, j), yblk)], cl_recv.at[j], 8, y_peer(j))
    spread(t_hbm, rt, 1)
    spread(b_hbm, bt, 5)

    wait_bytes(cy_recv.at[pl.ds(1, ny - 1)], recv_sem.at[0])
    mid = cy_send[rows(y, yblk), :].astype(F32)
    for j in range(1, ny):
        mid = mid + cy_recv[j].astype(F32)
    mid_w = wide(mid)
    share = dot(mid_w, wx[...])
    for i in range(lx):
        x_send[i] = share[:, i * rank:(i + 1) * rank].astype(BF)
    for j in far_first(nx):
        send(x_send.at[level_of(j)], x_recv.at[j], 6, x_peer(j))
    zs_send[0] = mid.astype(BF)
    if lz > 1:
        zl = dot(mid_w, wzl[...])
        for i in range(lz - 1):
            zs_send[i + 1] = zl[:, i * rank:(i + 1) * rank].astype(BF)
    for j in far_first(nz):
        send(zs_send.at[level_of(j)], zs_recv.at[j], 4, z_peer(j))
    send(h_send, h_recv, 2, y_peer(1))

    loads["b"].wait()
    vx[...] = down(climb(ly + lz, lx), ly + lz, lx)
    vz[...] = down(tz, ly, lz)

    wait_bytes(x_recv.at[pl.ds(1, nx - 1)], recv_sem.at[6])
    parts = [x_recv[1]]
    for level in range(1, lx):
        parts.append(wide(functools.reduce(jnp.add, [x_recv[j].astype(F32) for j in range(1 << level, 2 << level)])))
    top = dot(jnp.concatenate(parts, axis=1), vx[...])
    cz_send[...] = top.astype(BF)
    for j in far_first(nz):
        send(cz_send, cz_recv.at[j], 3, z_peer(j))

    rt[0] = tv[1]
    rt[5] = tv[2]
    bt[0] = bv[1]
    bt[5] = bv[2]
    wait_bytes(rt.at[pl.ds(1, 4)], recv_sem.at[1])
    lifts = []
    for quad in range(2):
        both = jnp.concatenate([rt[2 * quad], rt[2 * quad + 1]], axis=0)
        lifts.append(dot(both, rt[5 - quad]))
    lifts = jnp.concatenate(lifts, axis=0)
    whole = dot(wide(lifts), wx[:, :rank])
    for r in range(4):
        at = slice(r * rank, (r + 1) * rank)
        vw[:, at] = up_weight(lifts[at].T)
        vg[:, at] = up_weight(whole[at].T)
    wait_bytes(zs_recv.at[pl.ds(1, nz - 1)], recv_sem.at[4])
    parts = [zs_recv[1]]
    for level in range(1, lz):
        parts.append(wide(functools.reduce(jnp.add, [zs_recv[j].astype(F32) for j in range(1 << level, 2 << level)])))
    mid_far = dot(jnp.concatenate(parts, axis=1), vz[...])

    wait_bytes(cl_recv.at[pl.ds(1, ny - 1)], recv_sem.at[8])
    given = [cl_send[rows(y, yblk), :]] + [cl_recv[j] for j in range(1, ny)]
    sums = [given[2 * r].astype(F32) + given[2 * r + 1].astype(F32) for r in range(4)]
    quads = []
    for quad in range(2):
        left = jnp.concatenate([*split(sums[2 * quad]), *split(sums[2 * quad + 1])], axis=1)
        right = [rt[2 * quad]] * 2 + [rt[2 * quad + 1]] * 2
        quads.append(dot(left, jnp.concatenate(right, axis=0)))
    wait_bytes(bt.at[pl.ds(1, 4)], recv_sem.at[5])
    local = []
    for quad in range(2):
        both = jnp.concatenate([rt[2 * quad], rt[2 * quad + 1]], axis=0)
        high, low = split(dot(both, bt[5 - quad]))
        seen = dot_nt(wide(quads[1 - quad]), jnp.concatenate([high, high, low], axis=1))
        for half in range(2):
            r = 2 * quad + half
            sibling = jnp.concatenate(split(sums[r ^ 1]), axis=1)
            local.append(seen[:, half * rank:(half + 1) * rank] + dot_nt(sibling, jnp.concatenate([bt[r]] * 2, axis=1)))
    local = jnp.concatenate(local, axis=1) + dot(wide(mid_far), vw[...])

    wait_bytes(cz_recv.at[pl.ds(1, nz - 1)], recv_sem.at[3])
    for j in range(1, nz):
        top = top + cz_recv[j].astype(F32)
    pair_far = (local + dot(wide(top), vg[...])).astype(BF)
    for r in range(4):
        far_y_send[r] = pair_far[:, r * rank:(r + 1) * rank]
    for j in far_first(ny):
        send(far_y_send.at[j // 2], far_y.at[rows(y, yblk)], 7, y_peer(j))
    far_y[rows(y, yblk), :] = far_y_send[0]

    wait_bytes(h_recv, recv_sem.at[2])
    far = dot_nt(h_recv[...], bv[0]).astype(BF)
    near_part(1, 2)
    near[...] += dot_nt(uv[...], far)
    wait_bytes(far_y.at[pl.ds(0, (ny - 1) * yblk)], recv_sem.at[7])
    far_out[...] = far_y[...]

    wait_bytes(cy_recv.at[pl.ds(1, ny - 1)], send_sem.at[0])
    wait_bytes(rt.at[pl.ds(1, 4)], send_sem.at[1])
    wait_bytes(h_send, send_sem.at[2])
    wait_bytes(cz_recv.at[pl.ds(1, nz - 1)], send_sem.at[3])
    wait_bytes(zs_recv.at[pl.ds(1, nz - 1)], send_sem.at[4])
    wait_bytes(bt.at[pl.ds(1, 4)], send_sem.at[5])
    wait_bytes(x_recv.at[pl.ds(1, nx - 1)], send_sem.at[6])
    wait_bytes(far_y.at[pl.ds(0, (ny - 1) * yblk)], send_sem.at[7])
    wait_bytes(cl_recv.at[pl.ds(1, ny - 1)], send_sem.at[8])


def last_kernel(near, lift, far, o_hbm, far_t, ov, store_sem):
    leaf = near.shape[0]
    chunks = store_sem.shape[0]
    tile = leaf // chunks
    far_t[...] = jnp.concatenate([far[...].T] * 2, axis=0)
    stores = []
    for step in range(chunks):
        at = pl.ds(step * tile, tile)
        ov[at, :] = (near[at, :] + dot(lift[at, :], far_t[...])).astype(BF)
        store = pltpu.make_async_copy(ov.at[at], o_hbm.at[at], store_sem.at[step])
        store.start()
        stores.append(store)
    for store in stores:
        store.wait()


def solution(mesh):
    ly = 3
    lz = mesh.shape["sub"].bit_length() - 1 - ly
    lx = mesh.shape["grp"].bit_length() - 1
    ny, nz, nx = 1 << ly, 1 << lz, 1 << lx

    def body(vectors, blocks, basis, transfer, coupling):
        leaf, vecs = vectors.shape[2:]
        rank = basis.shape[3]
        levels = transfer.shape[2]
        yblk = vecs // ny
        scratch = [
            pltpu.VMEM((leaf, vecs), BF),
            pltpu.VMEM((leaf, leaf), BF),
            pltpu.VMEM((leaf, rank), BF),
            pltpu.VMEM((rank, leaf), BF),
            pltpu.VMEM((levels, rank, rank), BF),
            pltpu.VMEM((levels, rank, rank), BF),
            pltpu.VMEM((6, rank, rank), BF),
            pltpu.VMEM((6, rank, rank), BF),
            pltpu.VMEM((3 * rank, rank), BF),
            pltpu.VMEM((3 * rank, lx * rank), BF),
            pltpu.VMEM((3 * rank, max(1, lz - 1) * rank), BF),
            pltpu.VMEM(((3 * lx - 2) * rank, rank), BF),
            pltpu.VMEM(((3 * lz - 2) * rank, rank), BF),
            pltpu.VMEM((3 * rank, 4 * rank), BF),
            pltpu.VMEM((3 * rank, 4 * rank), BF),
            pltpu.VMEM((vecs, rank), BF),
            pltpu.VMEM((vecs, rank), BF),
            pltpu.VMEM((vecs, rank), BF),
            pltpu.VMEM((ny, yblk, rank), BF),
            pltpu.VMEM((vecs, rank), BF),
            pltpu.VMEM((ny, yblk, rank), BF),
            pltpu.VMEM((yblk, rank), BF),
            pltpu.VMEM((nz, yblk, rank), BF),
            pltpu.VMEM((lz, yblk, rank), BF),
            pltpu.VMEM((nz, yblk, rank), BF),
            pltpu.VMEM((lx, yblk, rank), BF),
            pltpu.VMEM((nx, yblk, rank), BF),
            pltpu.VMEM((4, yblk, rank), BF),
            pltpu.VMEM((vecs, rank), BF),
            pltpu.SemaphoreType.DMA((6,)),
            pltpu.SemaphoreType.DMA((9,)),
            pltpu.SemaphoreType.DMA((9,)),
        ]
        vmem = pl.BlockSpec(memory_space=pltpu.VMEM)
        near, lift, far = pl.pallas_call(
            functools.partial(kernel, (lz, lx)),
            out_shape=[
                jax.ShapeDtypeStruct((leaf, vecs), F32),
                jax.ShapeDtypeStruct((leaf, 2 * rank), BF),
                jax.ShapeDtypeStruct((vecs, rank), BF),
            ],
            in_specs=[pl.BlockSpec(memory_space=pltpu.HBM)] * 5,
            out_specs=[vmem] * 3,
            scratch_shapes=scratch,
            compiler_params=pltpu.CompilerParams(
                collective_id=0, has_side_effects=True, vmem_limit_bytes=32 * 1024 * 1024,
            ),
        )(*(pltpu.with_memory_space_constraint(whole[0, 0], pltpu.HBM) for whole in (vectors, blocks, basis, transfer, coupling)))
        out = pl.pallas_call(
            last_kernel,
            out_shape=jax.ShapeDtypeStruct((leaf, vecs), BF),
            in_specs=[vmem] * 3,
            out_specs=pl.BlockSpec(memory_space=pltpu.HBM),
            scratch_shapes=[
                pltpu.VMEM((2 * rank, vecs), BF),
                pltpu.VMEM((leaf, vecs), BF),
                pltpu.SemaphoreType.DMA((4,)),
            ],
            compiler_params=pltpu.CompilerParams(vmem_limit_bytes=24 * 1024 * 1024),
        )(near, lift, far)
        return out[None, None]

    return jax.shard_map(
        body,
        mesh=mesh,
        in_specs=(
            P("grp", "sub", None, None),
            P("grp", "sub", None, None),
            P("grp", "sub", None, None),
            P("grp", "sub", None, None, None),
            P("grp", "sub", None, None, None),
        ),
        out_specs=P("grp", "sub", None, None),
        check_vma=False,
    )
```

profile of v0, /device:TPU:1, one launch (start us, length us, event | category | flops | bytes accessed | tf_op | source)
XLA Modules:
  0.0 38.0 jit_solution(10794867240924520954)
XLA Ops:
  0.0 36.7 %shard_map.55 = (f32[1024,512]{1,0:T(8,128)S(1)}, bf16[1024,256]{1,0:T(8,128)(2,1)S(1)}, bf16[512,128]{1,0:T(8,128)(2,1)S(1)}) custom-call(bf16[1024,512]{1,0:T(8,128)(2,1)} %bitcast.7, bf16[1024,1024]{1,0:T(8,128)(2,1)} %bitcast.6, bf16[1024,128]{1,0:T(8,128)(2,1)} %bitcast.10, bf16[9,128,128]{2,1,0:T(8,128)(2,1)} %bitcast.8, bf16[9,128,128]{2,1,0:T(8,128)(2,1)} %bitcast.9), custom_call_target="tpu_custom_call" | custom-call | tf_op jit(solution)/shard_map/pallas_call | solution.py:347
  36.7 1.3 %shard_map.56 = bf16[1024,512]{1,0:T(8,128)(2,1)} custom-call(f32[1024,512]{1,0:T(8,128)S(1)} %get-tuple-element.8.near, bf16[1024,256]{1,0:T(8,128)(2,1)S(1)} %get-tuple-element.9.lift, bf16[512,128]{1,0:T(8,128)(2,1)S(1)} %get-tuple-element.10.far), custom_call_target="tpu_custom_call" | custom-call | tf_op jit(solution)/shard_map/pallas_call | solution.py:361
where the time goes:
time: 38.1 us; the launch traced here: 38 us
  Pallas kernels  38 us (100%)
    pallas_call x1, Pallas kernels, body(): pl.pallas_call(functools.partial(kernel, (lz, lx)), out_shape=[jax.ShapeD...  36.7 us
    pallas_call x1, Pallas kernels, body(): pl.pallas_call(last_kernel, out_shape=jax.ShapeDtypeStruct((leaf, vecs),...  1.31 us

commit v1 on v0

--- a/solution.py
+++ b/solution.py
@@ -74,7 +74,7 @@
            h_send, h_recv, cy_send, cy_recv, cl_send, cl_recv,
            cz_send, cz_recv, zs_send, zs_recv, x_send, x_recv,
            far_y_send, far_y,
-           load_sem, send_sem, recv_sem):
+           load_sem, y_sem, z_sem, send_sem, recv_sem):
     lz, lx = dims
     ly = 3
     ny, nz, nx = 1 << ly, 1 << lz, 1 << lx
@@ -102,12 +102,23 @@
             device_id=peer, device_id_type=MESH,
         ).start()
 
+    order = sorted(range(ny), key=lambda place: min(place, ny - place))
+    rank_y = sum(jnp.where(y == place, k, 0) for k, place in enumerate(order))
     barrier = pltpu.get_barrier_semaphore()
-    peers = []
-    for j in far_first(8):
-        peers += [peer(j) for peer, count in ((y_peer, ny), (z_peer, nz), (x_peer, nx)) if j < count]
-    for peer in peers:
-        pl.semaphore_signal(barrier, inc=1, device_id=peer, device_id_type=MESH)
+
+    def greet(sem, peer):
+        pl.semaphore_signal(sem, inc=1, device_id=peer, device_id_type=MESH)
+
+    for k, place in reversed(list(enumerate(order))):
+        @pl.when(rank_y < k)
+        def _():
+            greet(barrier, {"sub": z * ny + place})
+    for place in reversed(range(nz)):
+        @pl.when(z < place)
+        def _():
+            greet(barrier, {"sub": place * ny + y})
+    for j in far_first(nx):
+        greet(barrier, x_peer(j))
 
     head = leaf // 2
     loads = {}
@@ -122,6 +133,16 @@
         loads[name] = pltpu.make_async_copy(src, dst, load_sem.at[i])
         loads[name].start()
 
+    pl.semaphore_wait(barrier, nx - 1 + z + rank_y)
+    for k, place in enumerate(order):
+        @pl.when(rank_y > k)
+        def _():
+            greet(y_sem.at[y], {"sub": z * ny + place})
+    for place in range(nz):
+        @pl.when(z > place)
+        def _():
+            greet(z_sem, {"sub": place * ny + y})
+
     pair = lax.div(y, 2)
     outward = 2 * lax.rem(y, 2) - 1
 
@@ -163,9 +184,14 @@
     hat = (hat_t + dot(ut[:, head:], xv[head:, :])).T
     hat_w = wide(hat)
     cy_send[...] = dot(hat_w, wy[...]).astype(BF)
-    pl.semaphore_wait(barrier, len(peers))
-    for j in far_first(ny):
-        send(cy_send.at[rows(flip(y, j), yblk)], cy_recv.at[j], 0, y_peer(j))
+
+    def scatter(place):
+        send(cy_send.at[pl.ds(place * yblk, yblk)], cy_recv.at[flip(y, place)], 0, {"sub": z * ny + place})
+
+    for k, place in enumerate(order):
+        @pl.when(rank_y > k)
+        def _():
+            scatter(place)
 
     cl_send[...] = dot(hat_w[:, :2 * rank], jnp.concatenate([tv[0], tv[0]], axis=0)).astype(BF)
     h_send[...] = hat.astype(BF)
@@ -176,6 +202,11 @@
     lift_out[...] = jnp.concatenate(split(dot(uv[...], tv[0])), axis=1)
     loads["d"].wait()
     near_part(0, 2)
+    for k, place in enumerate(order):
+        @pl.when(rank_y < k)
+        def _():
+            pl.semaphore_wait(y_sem.at[place], 1)
+            scatter(place)
     for j in far_first(ny):
         send(cl_send.at[rows(flip(y, j), yblk)], cl_recv.at[j], 8, y_peer(j))
     spread(t_hbm, rt, 1)
@@ -196,6 +227,11 @@
         zl = dot(mid_w, wzl[...])
         for i in range(lz - 1):
             zs_send[i + 1] = zl[:, i * rank:(i + 1) * rank].astype(BF)
+
+    @pl.when(z < nz - 1)
+    def _():
+        pl.semaphore_wait(z_sem, nz - 1 - z)
+
     for j in far_first(nz):
         send(zs_send.at[level_of(j)], zs_recv.at[j], 4, z_peer(j))
     send(h_send, h_recv, 2, y_peer(1))
@@ -340,6 +376,8 @@
             pltpu.VMEM((4, yblk, rank), BF),
             pltpu.VMEM((vecs, rank), BF),
             pltpu.SemaphoreType.DMA((6,)),
+            pltpu.SemaphoreType.REGULAR((ny,)),
+            pltpu.SemaphoreType.REGULAR,
             pltpu.SemaphoreType.DMA((9,)),
             pltpu.SemaphoreType.DMA((9,)),
         ]

time: 38.1 us -> 39.6 us (1.039)
  Pallas kernels: 38 us -> 39.5 us
    pallas_call x1, Pallas kernels: 36.7 us -> 38.2 us  [body(): pl.pallas_call(functools.partial(kernel, (lz, lx)), out_shape=[jax.ShapeD...]
where the time goes in v1:
time: 39.6 us; the launch traced here: 39.5 us
  Pallas kernels  39.5 us (100%)
    pallas_call x1, Pallas kernels, body(): pl.pallas_call(functools.partial(kernel, (lz, lx)), out_shape=[jax.ShapeD...  38.2 us
    pallas_call x1, Pallas kernels, body(): pl.pallas_call(last_kernel, out_shape=jax.ShapeDtypeStruct((leaf, vecs),...  1.3 us

profile of v1, /device:TPU:1, one launch (start us, length us, event | category | flops | bytes accessed | tf_op | source)
XLA Modules:
  0.0 39.5 jit_solution(517372517464512152)
XLA Ops:
  0.0 38.2 %shard_map.55 = (f32[1024,512]{1,0:T(8,128)S(1)}, bf16[1024,256]{1,0:T(8,128)(2,1)S(1)}, bf16[512,128]{1,0:T(8,128)(2,1)S(1)}) custom-call(bf16[1024,512]{1,0:T(8,128)(2,1)} %bitcast.7, bf16[1024,1024]{1,0:T(8,128)(2,1)} %bitcast.6, bf16[1024,128]{1,0:T(8,128)(2,1)} %bitcast.10, bf16[9,128,128]{2,1,0:T(8,128)(2,1)} %bitcast.8, bf16[9,128,128]{2,1,0:T(8,128)(2,1)} %bitcast.9), custom_call_target="tpu_custom_call" | custom-call | tf_op jit(solution)/shard_map/pallas_call | solution.py:385
  38.2 1.3 %shard_map.56 = bf16[1024,512]{1,0:T(8,128)(2,1)} custom-call(f32[1024,512]{1,0:T(8,128)S(1)} %get-tuple-element.8.near, bf16[1024,256]{1,0:T(8,128)(2,1)S(1)} %get-tuple-element.9.lift, bf16[512,128]{1,0:T(8,128)(2,1)S(1)} %get-tuple-element.10.far), custom_call_target="tpu_custom_call" | custom-call | tf_op jit(solution)/shard_map/pallas_call | solution.py:399

commit v2 on v0

--- a/solution.py
+++ b/solution.py
@@ -45,6 +45,11 @@
     return [j for j in (4, 5, 3, 7, 6, 2, 1) if j < count]
 
 
+def early(count, cores):
+    ring = sorted(range(count), key=lambda place: min(place, count - place))
+    return [place * cores + core for place in ring for core in reversed(range(cores))]
+
+
 def wait_bytes(ref, sem):
     pltpu.make_async_copy(ref, ref, sem).wait()
 
@@ -74,7 +79,7 @@
            h_send, h_recv, cy_send, cy_recv, cl_send, cl_recv,
            cz_send, cz_recv, zs_send, zs_recv, x_send, x_recv,
            far_y_send, far_y,
-           load_sem, send_sem, recv_sem):
+           load_sem, z_sem, send_sem, recv_sem):
     lz, lx = dims
     ly = 3
     ny, nz, nx = 1 << ly, 1 << lz, 1 << lx
@@ -103,11 +108,18 @@
         ).start()
 
     barrier = pltpu.get_barrier_semaphore()
-    peers = []
-    for j in far_first(8):
-        peers += [peer(j) for peer, count in ((y_peer, ny), (z_peer, nz), (x_peer, nx)) if j < count]
-    for peer in peers:
-        pl.semaphore_signal(barrier, inc=1, device_id=peer, device_id_type=MESH)
+
+    def greet(sem, peer):
+        pl.semaphore_signal(sem, inc=1, device_id=peer, device_id_type=MESH)
+
+    for j in far_first(ny):
+        greet(barrier, y_peer(j))
+    for place in reversed(range(nz)):
+        @pl.when(z < place)
+        def _():
+            greet(barrier, {"sub": place * ny + y})
+    for j in far_first(nx):
+        greet(barrier, x_peer(j))
 
     head = leaf // 2
     loads = {}
@@ -163,7 +175,11 @@
     hat = (hat_t + dot(ut[:, head:], xv[head:, :])).T
     hat_w = wide(hat)
     cy_send[...] = dot(hat_w, wy[...]).astype(BF)
-    pl.semaphore_wait(barrier, len(peers))
+    pl.semaphore_wait(barrier, ny - 1 + nx - 1 + z)
+    for place in range(nz):
+        @pl.when(z > place)
+        def _():
+            greet(z_sem, {"sub": place * ny + y})
     for j in far_first(ny):
         send(cy_send.at[rows(flip(y, j), yblk)], cy_recv.at[j], 0, y_peer(j))
 
@@ -176,10 +192,8 @@
     lift_out[...] = jnp.concatenate(split(dot(uv[...], tv[0])), axis=1)
     loads["d"].wait()
     near_part(0, 2)
-    for j in far_first(ny):
-        send(cl_send.at[rows(flip(y, j), yblk)], cl_recv.at[j], 8, y_peer(j))
-    spread(t_hbm, rt, 1)
-    spread(b_hbm, bt, 5)
+    loads["b"].wait()
+    vx[...] = down(climb(ly + lz, lx), ly + lz, lx)
 
     wait_bytes(cy_recv.at[pl.ds(1, ny - 1)], recv_sem.at[0])
     mid = cy_send[rows(y, yblk), :].astype(F32)
@@ -189,20 +203,29 @@
     share = dot(mid_w, wx[...])
     for i in range(lx):
         x_send[i] = share[:, i * rank:(i + 1) * rank].astype(BF)
-    for j in far_first(nx):
-        send(x_send.at[level_of(j)], x_recv.at[j], 6, x_peer(j))
+    for place in early(nx // 2, 2):
+        @pl.when(grp != place)
+        def _():
+            apart = flip(grp, place)
+            level = sum(jnp.where(apart >= 1 << i, 1, 0) for i in range(1, lx))
+            send(x_send.at[level], x_recv.at[apart], 6, {"grp": place})
     zs_send[0] = mid.astype(BF)
     if lz > 1:
         zl = dot(mid_w, wzl[...])
         for i in range(lz - 1):
             zs_send[i + 1] = zl[:, i * rank:(i + 1) * rank].astype(BF)
+
+    @pl.when(z < nz - 1)
+    def _():
+        pl.semaphore_wait(z_sem, nz - 1 - z)
+
     for j in far_first(nz):
         send(zs_send.at[level_of(j)], zs_recv.at[j], 4, z_peer(j))
+    for j in far_first(ny):
+        send(cl_send.at[rows(flip(y, j), yblk)], cl_recv.at[j], 8, y_peer(j))
+    spread(t_hbm, rt, 1)
+    spread(b_hbm, bt, 5)
     send(h_send, h_recv, 2, y_peer(1))
-
-    loads["b"].wait()
-    vx[...] = down(climb(ly + lz, lx), ly + lz, lx)
-    vz[...] = down(tz, ly, lz)
 
     wait_bytes(x_recv.at[pl.ds(1, nx - 1)], recv_sem.at[6])
     parts = [x_recv[1]]
@@ -210,8 +233,12 @@
         parts.append(wide(functools.reduce(jnp.add, [x_recv[j].astype(F32) for j in range(1 << level, 2 << level)])))
     top = dot(jnp.concatenate(parts, axis=1), vx[...])
     cz_send[...] = top.astype(BF)
-    for j in far_first(nz):
-        send(cz_send, cz_recv.at[j], 3, z_peer(j))
+    for place in range(nz):
+        @pl.when(z != place)
+        def _():
+            send(cz_send, cz_recv.at[flip(z, place)], 3, {"sub": place * ny + y})
+
+    vz[...] = down(tz, ly, lz)
 
     rt[0] = tv[1]
     rt[5] = tv[2]
@@ -260,8 +287,10 @@
     pair_far = (local + dot(wide(top), vg[...])).astype(BF)
     for r in range(4):
         far_y_send[r] = pair_far[:, r * rank:(r + 1) * rank]
-    for j in far_first(ny):
-        send(far_y_send.at[j // 2], far_y.at[rows(y, yblk)], 7, y_peer(j))
+    for place in early(ny, 1):
+        @pl.when(y != place)
+        def _():
+            send(far_y_send.at[lax.div(flip(y, place), 2)], far_y.at[rows(y, yblk)], 7, {"sub": z * ny + place})
     far_y[rows(y, yblk), :] = far_y_send[0]
 
     wait_bytes(h_recv, recv_sem.at[2])
@@ -340,6 +369,7 @@
             pltpu.VMEM((4, yblk, rank), BF),
             pltpu.VMEM((vecs, rank), BF),
             pltpu.SemaphoreType.DMA((6,)),
+            pltpu.SemaphoreType.REGULAR,
             pltpu.SemaphoreType.DMA((9,)),
             pltpu.SemaphoreType.DMA((9,)),
         ]

time: 38.1 us -> 36.3 us (0.953); the launches traced: 38 us -> 35.7 us
  Pallas kernels: 38 us -> 35.7 us
    pallas_call x1, Pallas kernels: 36.7 us -> 34.4 us  [body(): pl.pallas_call(functools.partial(kernel, (lz, lx)), out_shape=[jax.ShapeD...]
where the time goes in v2:
time: 36.3 us; the launch traced here: 35.7 us
  Pallas kernels  35.7 us (98%)
    pallas_call x1, Pallas kernels, body(): pl.pallas_call(functools.partial(kernel, (lz, lx)), out_shape=[jax.ShapeD...  34.4 us
    pallas_call x1, Pallas kernels, body(): pl.pallas_call(last_kernel, out_shape=jax.ShapeDtypeStruct((leaf, vecs),...  1.3 us

profile of v2, /device:TPU:1, one launch (start us, length us, event | category | flops | bytes accessed | tf_op | source)
XLA Modules:
  0.0 35.7 jit_solution(10771005646144963771)
XLA Ops:
  0.0 34.4 %shard_map.55 = (f32[1024,512]{1,0:T(8,128)S(1)}, bf16[1024,256]{1,0:T(8,128)(2,1)S(1)}, bf16[512,128]{1,0:T(8,128)(2,1)S(1)}) custom-call(bf16[1024,512]{1,0:T(8,128)(2,1)} %bitcast.7, bf16[1024,1024]{1,0:T(8,128)(2,1)} %bitcast.6, bf16[1024,128]{1,0:T(8,128)(2,1)} %bitcast.10, bf16[9,128,128]{2,1,0:T(8,128)(2,1)} %bitcast.8, bf16[9,128,128]{2,1,0:T(8,128)(2,1)} %bitcast.9), custom_call_target="tpu_custom_call" | custom-call | tf_op jit(solution)/shard_map/pallas_call | solution.py:377
  34.4 1.3 %shard_map.56 = bf16[1024,512]{1,0:T(8,128)(2,1)} custom-call(f32[1024,512]{1,0:T(8,128)S(1)} %get-tuple-element.8.near, bf16[1024,256]{1,0:T(8,128)(2,1)S(1)} %get-tuple-element.9.lift, bf16[512,128]{1,0:T(8,128)(2,1)S(1)} %get-tuple-element.10.far), custom_call_target="tpu_custom_call" | custom-call | tf_op jit(solution)/shard_map/pallas_call | solution.py:391

commit v3 on v2

--- a/solution.py
+++ b/solution.py
@@ -10,6 +10,7 @@
 MESH = pl.DeviceIdType.MESH
 BF = jnp.bfloat16
 F32 = jnp.float32
+CHUNKS = 2
 
 
 def dot(left, right):
@@ -86,6 +87,7 @@
     leaf, vecs = x_hbm.shape
     rank = u_hbm.shape[1]
     yblk = vecs // ny
+    half = yblk // CHUNKS
     sub, grp = lax.axis_index("sub"), lax.axis_index("grp")
     y, z = lax.rem(sub, ny), lax.div(sub, ny)
 
@@ -100,12 +102,30 @@
 
     def rows(index, size):
         return pl.ds(pl.multiple_of(index * size, size), size)
+
+    def part(index, c):
+        return pl.ds(pl.multiple_of(index * yblk + c * half, half), half)
 
     def send(src, dst, group, peer):
         pltpu.make_async_remote_copy(
             src_ref=src, dst_ref=dst, send_sem=send_sem.at[group], recv_sem=recv_sem.at[group],
             device_id=peer, device_id_type=MESH,
         ).start()
+
+    head = leaf // 2
+    loads = {}
+    for i, (name, src, dst) in enumerate((
+        ("t", t_hbm.at[pl.ds(0, ly)], tv.at[pl.ds(0, ly)]),
+        ("u", u_hbm, uv),
+        ("x0", x_hbm.at[pl.ds(0, head)], xv.at[pl.ds(0, head)]),
+        ("x1", x_hbm.at[pl.ds(head, head)], xv.at[pl.ds(head, head)]),
+        ("t1", t_hbm.at[pl.ds(ly, lz + lx)], tv.at[pl.ds(ly, lz + lx)]),
+        ("b", b_hbm, bv),
+        ("d", d_hbm, dv),
+    )):
+        loads[name] = pltpu.make_async_copy(src, dst, load_sem.at[i])
+    for name in ("t", "u", "x0", "x1"):
+        loads[name].start()
 
     barrier = pltpu.get_barrier_semaphore()
 
@@ -121,19 +141,6 @@
     for j in far_first(nx):
         greet(barrier, x_peer(j))
 
-    head = leaf // 2
-    loads = {}
-    for i, (name, src, dst) in enumerate((
-        ("u", u_hbm, uv),
-        ("x0", x_hbm.at[pl.ds(0, head)], xv.at[pl.ds(0, head)]),
-        ("x1", x_hbm.at[pl.ds(head, head)], xv.at[pl.ds(head, head)]),
-        ("t", t_hbm, tv),
-        ("d", d_hbm, dv),
-        ("b", b_hbm, bv),
-    )):
-        loads[name] = pltpu.make_async_copy(src, dst, load_sem.at[i])
-        loads[name].start()
-
     pair = lax.div(y, 2)
     outward = 2 * lax.rem(y, 2) - 1
 
@@ -172,19 +179,23 @@
     loads["x0"].wait()
     hat_t = dot(ut[:, :head], xv[:head, :])
     loads["x1"].wait()
+    for name in ("t1", "b", "d"):
+        loads[name].start()
     hat = (hat_t + dot(ut[:, head:], xv[head:, :])).T
     hat_w = wide(hat)
     cy_send[...] = dot(hat_w, wy[...]).astype(BF)
     pl.semaphore_wait(barrier, ny - 1 + nx - 1 + z)
+    for c in range(CHUNKS):
+        for j in far_first(ny):
+            send(cy_send.at[part(flip(y, j), c)], cy_recv.at[c, j], 5 + c, y_peer(j))
     for place in range(nz):
         @pl.when(z > place)
         def _():
             greet(z_sem, {"sub": place * ny + y})
-    for j in far_first(ny):
-        send(cy_send.at[rows(flip(y, j), yblk)], cy_recv.at[j], 0, y_peer(j))
 
     cl_send[...] = dot(hat_w[:, :2 * rank], jnp.concatenate([tv[0], tv[0]], axis=0)).astype(BF)
     h_send[...] = hat.astype(BF)
+    loads["t1"].wait()
     tz = climb(ly, lz + lx - 1)
     wx[...] = jnp.concatenate([up_weight(product) for product in tz[lz - 1:]], axis=1)
     if lz > 1:
@@ -195,21 +206,25 @@
     loads["b"].wait()
     vx[...] = down(climb(ly + lz, lx), ly + lz, lx)
 
-    wait_bytes(cy_recv.at[pl.ds(1, ny - 1)], recv_sem.at[0])
-    mid = cy_send[rows(y, yblk), :].astype(F32)
-    for j in range(1, ny):
-        mid = mid + cy_recv[j].astype(F32)
-    mid_w = wide(mid)
-    share = dot(mid_w, wx[...])
-    for i in range(lx):
-        x_send[i] = share[:, i * rank:(i + 1) * rank].astype(BF)
-    for place in early(nx // 2, 2):
-        @pl.when(grp != place)
-        def _():
-            apart = flip(grp, place)
-            level = sum(jnp.where(apart >= 1 << i, 1, 0) for i in range(1, lx))
-            send(x_send.at[level], x_recv.at[apart], 6, {"grp": place})
-    zs_send[0] = mid.astype(BF)
+    mids = []
+    for c in range(CHUNKS):
+        wait_bytes(cy_recv.at[c, pl.ds(1, ny - 1)], recv_sem.at[5 + c])
+        mid = cy_send[part(y, c), :].astype(F32)
+        for j in range(1, ny):
+            mid = mid + cy_recv[c, j].astype(F32)
+        mids.append(wide(mid))
+        share = dot(mids[c], wx[...])
+        for i in range(lx):
+            x_send[c, i] = share[:, i * rank:(i + 1) * rank].astype(BF)
+        for place in early(nx // 2, 2):
+            @pl.when(grp != place)
+            def _():
+                apart = flip(grp, place)
+                level = sum(jnp.where(apart >= 1 << i, 1, 0) for i in range(1, lx))
+                send(x_send.at[c, level], x_recv.at[c, apart], 7 + c, {"grp": place})
+
+    mid_w = jnp.concatenate(mids, axis=0)
+    zs_send[0] = mid_w[:, :rank]
     if lz > 1:
         zl = dot(mid_w, wzl[...])
         for i in range(lz - 1):
@@ -221,23 +236,26 @@
 
     for j in far_first(nz):
         send(zs_send.at[level_of(j)], zs_recv.at[j], 4, z_peer(j))
+
+    tops = []
+    for c in range(CHUNKS):
+        wait_bytes(x_recv.at[c, pl.ds(1, nx - 1)], recv_sem.at[7 + c])
+        parts = [x_recv[c, 1]]
+        for level in range(1, lx):
+            parts.append(wide(functools.reduce(jnp.add, [x_recv[c, j].astype(F32) for j in range(1 << level, 2 << level)])))
+        top = dot(jnp.concatenate(parts, axis=1), vx[...])
+        tops.append(top)
+        cz_send[c] = top.astype(BF)
+        for place in range(nz):
+            @pl.when(z != place)
+            def _():
+                send(cz_send.at[c], cz_recv.at[c, flip(z, place)], 9 + c, {"sub": place * ny + y})
+
     for j in far_first(ny):
-        send(cl_send.at[rows(flip(y, j), yblk)], cl_recv.at[j], 8, y_peer(j))
+        send(cl_send.at[rows(flip(y, j), yblk)], cl_recv.at[j], 0, y_peer(j))
     spread(t_hbm, rt, 1)
-    spread(b_hbm, bt, 5)
+    spread(b_hbm, bt, 3)
     send(h_send, h_recv, 2, y_peer(1))
-
-    wait_bytes(x_recv.at[pl.ds(1, nx - 1)], recv_sem.at[6])
-    parts = [x_recv[1]]
-    for level in range(1, lx):
-        parts.append(wide(functools.reduce(jnp.add, [x_recv[j].astype(F32) for j in range(1 << level, 2 << level)])))
-    top = dot(jnp.concatenate(parts, axis=1), vx[...])
-    cz_send[...] = top.astype(BF)
-    for place in range(nz):
-        @pl.when(z != place)
-        def _():
-            send(cz_send, cz_recv.at[flip(z, place)], 3, {"sub": place * ny + y})
-
     vz[...] = down(tz, ly, lz)
 
     rt[0] = tv[1]
@@ -261,7 +279,7 @@
         parts.append(wide(functools.reduce(jnp.add, [zs_recv[j].astype(F32) for j in range(1 << level, 2 << level)])))
     mid_far = dot(jnp.concatenate(parts, axis=1), vz[...])
 
-    wait_bytes(cl_recv.at[pl.ds(1, ny - 1)], recv_sem.at[8])
+    wait_bytes(cl_recv.at[pl.ds(1, ny - 1)], recv_sem.at[0])
     given = [cl_send[rows(y, yblk), :]] + [cl_recv[j] for j in range(1, ny)]
     sums = [given[2 * r].astype(F32) + given[2 * r + 1].astype(F32) for r in range(4)]
     quads = []
@@ -269,46 +287,51 @@
         left = jnp.concatenate([*split(sums[2 * quad]), *split(sums[2 * quad + 1])], axis=1)
         right = [rt[2 * quad]] * 2 + [rt[2 * quad + 1]] * 2
         quads.append(dot(left, jnp.concatenate(right, axis=0)))
-    wait_bytes(bt.at[pl.ds(1, 4)], recv_sem.at[5])
+    wait_bytes(bt.at[pl.ds(1, 4)], recv_sem.at[3])
     local = []
     for quad in range(2):
         both = jnp.concatenate([rt[2 * quad], rt[2 * quad + 1]], axis=0)
         high, low = split(dot(both, bt[5 - quad]))
         seen = dot_nt(wide(quads[1 - quad]), jnp.concatenate([high, high, low], axis=1))
-        for half in range(2):
-            r = 2 * quad + half
+        for side in range(2):
+            r = 2 * quad + side
             sibling = jnp.concatenate(split(sums[r ^ 1]), axis=1)
-            local.append(seen[:, half * rank:(half + 1) * rank] + dot_nt(sibling, jnp.concatenate([bt[r]] * 2, axis=1)))
+            local.append(seen[:, side * rank:(side + 1) * rank] + dot_nt(sibling, jnp.concatenate([bt[r]] * 2, axis=1)))
     local = jnp.concatenate(local, axis=1) + dot(wide(mid_far), vw[...])
 
-    wait_bytes(cz_recv.at[pl.ds(1, nz - 1)], recv_sem.at[3])
-    for j in range(1, nz):
-        top = top + cz_recv[j].astype(F32)
-    pair_far = (local + dot(wide(top), vg[...])).astype(BF)
-    for r in range(4):
-        far_y_send[r] = pair_far[:, r * rank:(r + 1) * rank]
-    for place in early(ny, 1):
-        @pl.when(y != place)
-        def _():
-            send(far_y_send.at[lax.div(flip(y, place), 2)], far_y.at[rows(y, yblk)], 7, {"sub": z * ny + place})
-    far_y[rows(y, yblk), :] = far_y_send[0]
+    for c in range(CHUNKS):
+        wait_bytes(cz_recv.at[c, pl.ds(1, nz - 1)], recv_sem.at[9 + c])
+        top = tops[c]
+        for j in range(1, nz):
+            top = top + cz_recv[c, j].astype(F32)
+        at = pl.ds(c * half, half)
+        pair_far = (local[c * half:(c + 1) * half] + dot(wide(top), vg[...])).astype(BF)
+        for r in range(4):
+            far_y_send[r, at, :] = pair_far[:, r * rank:(r + 1) * rank]
+        for place in early(ny, 1):
+            @pl.when(y != place)
+            def _():
+                send(far_y_send.at[lax.div(flip(y, place), 2), at], far_y.at[part(y, c)], 11 + c, {"sub": z * ny + place})
+        far_y[part(y, c), :] = far_y_send[0, at, :]
 
     wait_bytes(h_recv, recv_sem.at[2])
     far = dot_nt(h_recv[...], bv[0]).astype(BF)
     near_part(1, 2)
     near[...] += dot_nt(uv[...], far)
-    wait_bytes(far_y.at[pl.ds(0, (ny - 1) * yblk)], recv_sem.at[7])
+    for c in range(CHUNKS):
+        wait_bytes(far_y.at[pl.ds(0, (ny - 1) * half)], recv_sem.at[11 + c])
     far_out[...] = far_y[...]
 
-    wait_bytes(cy_recv.at[pl.ds(1, ny - 1)], send_sem.at[0])
+    wait_bytes(cl_recv.at[pl.ds(1, ny - 1)], send_sem.at[0])
     wait_bytes(rt.at[pl.ds(1, 4)], send_sem.at[1])
     wait_bytes(h_send, send_sem.at[2])
-    wait_bytes(cz_recv.at[pl.ds(1, nz - 1)], send_sem.at[3])
+    wait_bytes(bt.at[pl.ds(1, 4)], send_sem.at[3])
     wait_bytes(zs_recv.at[pl.ds(1, nz - 1)], send_sem.at[4])
-    wait_bytes(bt.at[pl.ds(1, 4)], send_sem.at[5])
-    wait_bytes(x_recv.at[pl.ds(1, nx - 1)], send_sem.at[6])
-    wait_bytes(far_y.at[pl.ds(0, (ny - 1) * yblk)], send_sem.at[7])
-    wait_bytes(cl_recv.at[pl.ds(1, ny - 1)], send_sem.at[8])
+    for c in range(CHUNKS):
+        wait_bytes(cy_recv.at[c, pl.ds(1, ny - 1)], send_sem.at[5 + c])
+        wait_bytes(x_recv.at[c, pl.ds(1, nx - 1)], send_sem.at[7 + c])
+        wait_bytes(cz_recv.at[c, pl.ds(1, nz - 1)], send_sem.at[9 + c])
+        wait_bytes(far_y.at[pl.ds(0, (ny - 1) * half)], send_sem.at[11 + c])
 
 
 def last_kernel(near, lift, far, o_hbm, far_t, ov, store_sem):
@@ -357,21 +380,21 @@
             pltpu.VMEM((vecs, rank), BF),
             pltpu.VMEM((vecs, rank), BF),
             pltpu.VMEM((vecs, rank), BF),
-            pltpu.VMEM((ny, yblk, rank), BF),
+            pltpu.VMEM((CHUNKS, ny, yblk // CHUNKS, rank), BF),
             pltpu.VMEM((vecs, rank), BF),
             pltpu.VMEM((ny, yblk, rank), BF),
-            pltpu.VMEM((yblk, rank), BF),
-            pltpu.VMEM((nz, yblk, rank), BF),
+            pltpu.VMEM((CHUNKS, yblk // CHUNKS, rank), BF),
+            pltpu.VMEM((CHUNKS, nz, yblk // CHUNKS, rank), BF),
             pltpu.VMEM((lz, yblk, rank), BF),
             pltpu.VMEM((nz, yblk, rank), BF),
-            pltpu.VMEM((lx, yblk, rank), BF),
-            pltpu.VMEM((nx, yblk, rank), BF),
+            pltpu.VMEM((CHUNKS, lx, yblk // CHUNKS, rank), BF),
+            pltpu.VMEM((CHUNKS, nx, yblk // CHUNKS, rank), BF),
             pltpu.VMEM((4, yblk, rank), BF),
             pltpu.VMEM((vecs, rank), BF),
-            pltpu.SemaphoreType.DMA((6,)),
+            pltpu.SemaphoreType.DMA((7,)),
             pltpu.SemaphoreType.REGULAR,
-            pltpu.SemaphoreType.DMA((9,)),
-            pltpu.SemaphoreType.DMA((9,)),
+            pltpu.SemaphoreType.DMA((13,)),
+            pltpu.SemaphoreType.DMA((13,)),
         ]
         vmem = pl.BlockSpec(memory_space=pltpu.VMEM)
         near, lift, far = pl.pallas_call(

time: 36.3 us -> 38.6 us (1.063); the launches traced: 35.7 us -> 38.4 us
  Pallas kernels: 35.7 us -> 38.4 us
    pallas_call x1, Pallas kernels: 34.4 us -> 37.1 us  [body(): pl.pallas_call(functools.partial(kernel, (lz, lx)), out_shape=[jax.ShapeD...]
where the time goes in v3:
time: 38.6 us; the launch traced here: 38.4 us
  Pallas kernels  38.4 us (99%)
    pallas_call x1, Pallas kernels, body(): pl.pallas_call(functools.partial(kernel, (lz, lx)), out_shape=[jax.ShapeD...  37.1 us
    pallas_call x1, Pallas kernels, body(): pl.pallas_call(last_kernel, out_shape=jax.ShapeDtypeStruct((leaf, vecs),...  1.31 us

profile of v3, /device:TPU:1, one launch (start us, length us, event | category | flops | bytes accessed | tf_op | source)
XLA Modules:
  0.0 38.4 jit_solution(15232094590606033312)
XLA Ops:
  0.0 37.1 %shard_map.55 = (f32[1024,512]{1,0:T(8,128)S(1)}, bf16[1024,256]{1,0:T(8,128)(2,1)S(1)}, bf16[512,128]{1,0:T(8,128)(2,1)S(1)}) custom-call(bf16[1024,512]{1,0:T(8,128)(2,1)} %bitcast.7, bf16[1024,1024]{1,0:T(8,128)(2,1)} %bitcast.6, bf16[1024,128]{1,0:T(8,128)(2,1)} %bitcast.10, bf16[9,128,128]{2,1,0:T(8,128)(2,1)} %bitcast.8, bf16[9,128,128]{2,1,0:T(8,128)(2,1)} %bitcast.9), custom_call_target="tpu_custom_call" | custom-call | tf_op jit(solution)/shard_map/pallas_call | solution.py:400
  37.1 1.3 %shard_map.56 = bf16[1024,512]{1,0:T(8,128)(2,1)} custom-call(f32[1024,512]{1,0:T(8,128)S(1)} %get-tuple-element.8.near, bf16[1024,256]{1,0:T(8,128)(2,1)S(1)} %get-tuple-element.9.lift, bf16[512,128]{1,0:T(8,128)(2,1)S(1)} %get-tuple-element.10.far), custom_call_target="tpu_custom_call" | custom-call | tf_op jit(solution)/shard_map/pallas_call | solution.py:414

commit v4 on v3

--- a/solution.py
+++ b/solution.py
@@ -10,7 +10,7 @@
 MESH = pl.DeviceIdType.MESH
 BF = jnp.bfloat16
 F32 = jnp.float32
-CHUNKS = 2
+CHUNKS = 1
 
 
 def dot(left, right):
@@ -236,6 +236,8 @@
 
     for j in far_first(nz):
         send(zs_send.at[level_of(j)], zs_recv.at[j], 4, z_peer(j))
+    for j in far_first(ny):
+        send(cl_send.at[rows(flip(y, j), yblk)], cl_recv.at[j], 0, y_peer(j))
 
     tops = []
     for c in range(CHUNKS):
@@ -251,8 +253,6 @@
             def _():
                 send(cz_send.at[c], cz_recv.at[c, flip(z, place)], 9 + c, {"sub": place * ny + y})
 
-    for j in far_first(ny):
-        send(cl_send.at[rows(flip(y, j), yblk)], cl_recv.at[j], 0, y_peer(j))
     spread(t_hbm, rt, 1)
     spread(b_hbm, bt, 3)
     send(h_send, h_recv, 2, y_peer(1))

time: 38.6 us -> 36.8 us (0.953)
  the two profiles are of different devices: /device:TPU:1 before, /device:TPU:16 now
where the time goes in v4:
time: 36.8 us; the launch traced here: 36.6 us
  Pallas kernels  36.6 us (99%)
    pallas_call x1, Pallas kernels, body(): pl.pallas_call(functools.partial(kernel, (lz, lx)), out_shape=[jax.ShapeD...  35.3 us
    pallas_call x1, Pallas kernels, body(): pl.pallas_call(last_kernel, out_shape=jax.ShapeDtypeStruct((leaf, vecs),...  1.31 us

profile of v4, /device:TPU:16, one launch (start us, length us, event | category | flops | bytes accessed | tf_op | source)
XLA Modules:
  0.0 36.6 jit_solution(12641160013778019659)
XLA Ops:
  0.0 35.3 %shard_map.55 = (f32[1024,512]{1,0:T(8,128)S(1)}, bf16[1024,256]{1,0:T(8,128)(2,1)S(1)}, bf16[512,128]{1,0:T(8,128)(2,1)S(1)}) custom-call(bf16[1024,512]{1,0:T(8,128)(2,1)} %bitcast.7, bf16[1024,1024]{1,0:T(8,128)(2,1)} %bitcast.6, bf16[1024,128]{1,0:T(8,128)(2,1)} %bitcast.10, bf16[9,128,128]{2,1,0:T(8,128)(2,1)} %bitcast.8, bf16[9,128,128]{2,1,0:T(8,128)(2,1)} %bitcast.9), custom_call_target="tpu_custom_call" | custom-call | tf_op jit(solution)/shard_map/pallas_call | solution.py:400
  35.3 1.3 %shard_map.56 = bf16[1024,512]{1,0:T(8,128)(2,1)} custom-call(f32[1024,512]{1,0:T(8,128)S(1)} %get-tuple-element.8.near, bf16[1024,256]{1,0:T(8,128)(2,1)S(1)} %get-tuple-element.9.lift, bf16[512,128]{1,0:T(8,128)(2,1)S(1)} %get-tuple-element.10.far), custom_call_target="tpu_custom_call" | custom-call | tf_op jit(solution)/shard_map/pallas_call | solution.py:414

commit v5 on v4

--- a/solution.py
+++ b/solution.py
@@ -46,9 +46,8 @@
     return [j for j in (4, 5, 3, 7, 6, 2, 1) if j < count]
 
 
-def early(count, cores):
-    ring = sorted(range(count), key=lambda place: min(place, count - place))
-    return [place * cores + core for place in ring for core in reversed(range(cores))]
+def later(index, k):
+    return jnp.where(index > k, 0, 1)
 
 
 def wait_bytes(ref, sem):
@@ -127,6 +126,8 @@
     for name in ("t", "u", "x0", "x1"):
         loads[name].start()
 
+    order = sorted(range(ny), key=lambda place: min(place, ny - place))
+    rank_y = sum(jnp.where(y == place, k, 0) for k, place in enumerate(order))
     barrier = pltpu.get_barrier_semaphore()
 
     def greet(sem, peer):
@@ -193,16 +194,9 @@
         def _():
             greet(z_sem, {"sub": place * ny + y})
 
-    cl_send[...] = dot(hat_w[:, :2 * rank], jnp.concatenate([tv[0], tv[0]], axis=0)).astype(BF)
-    h_send[...] = hat.astype(BF)
     loads["t1"].wait()
     tz = climb(ly, lz + lx - 1)
     wx[...] = jnp.concatenate([up_weight(product) for product in tz[lz - 1:]], axis=1)
-    if lz > 1:
-        wzl[...] = jnp.concatenate([up_exact(tv[ly])] + [up_weight(tz[i]) for i in range(1, lz - 1)], axis=1)
-    lift_out[...] = jnp.concatenate(split(dot(uv[...], tv[0])), axis=1)
-    loads["d"].wait()
-    near_part(0, 2)
     loads["b"].wait()
     vx[...] = down(climb(ly + lz, lx), ly + lz, lx)
 
@@ -216,16 +210,14 @@
         share = dot(mids[c], wx[...])
         for i in range(lx):
             x_send[c, i] = share[:, i * rank:(i + 1) * rank].astype(BF)
-        for place in early(nx // 2, 2):
-            @pl.when(grp != place)
-            def _():
-                apart = flip(grp, place)
-                level = sum(jnp.where(apart >= 1 << i, 1, 0) for i in range(1, lx))
-                send(x_send.at[c, level], x_recv.at[c, apart], 7 + c, {"grp": place})
+        for j in (4, 5, 6, 7, 2, 3, 1):
+            if j < nx:
+                send(x_send.at[c, level_of(j)], x_recv.at[c, j], 7 + c, x_peer(j))
 
     mid_w = jnp.concatenate(mids, axis=0)
     zs_send[0] = mid_w[:, :rank]
     if lz > 1:
+        wzl[...] = jnp.concatenate([up_exact(tv[ly])] + [up_weight(tz[i]) for i in range(1, lz - 1)], axis=1)
         zl = dot(mid_w, wzl[...])
         for i in range(lz - 1):
             zs_send[i + 1] = zl[:, i * rank:(i + 1) * rank].astype(BF)
@@ -236,28 +228,30 @@
 
     for j in far_first(nz):
         send(zs_send.at[level_of(j)], zs_recv.at[j], 4, z_peer(j))
+    cl_send[...] = dot(hat_w[:, :2 * rank], jnp.concatenate([tv[0], tv[0]], axis=0)).astype(BF)
+    h_send[...] = hat.astype(BF)
     for j in far_first(ny):
         send(cl_send.at[rows(flip(y, j), yblk)], cl_recv.at[j], 0, y_peer(j))
 
-    tops = []
     for c in range(CHUNKS):
         wait_bytes(x_recv.at[c, pl.ds(1, nx - 1)], recv_sem.at[7 + c])
         parts = [x_recv[c, 1]]
         for level in range(1, lx):
             parts.append(wide(functools.reduce(jnp.add, [x_recv[c, j].astype(F32) for j in range(1 << level, 2 << level)])))
         top = dot(jnp.concatenate(parts, axis=1), vx[...])
-        tops.append(top)
         cz_send[c] = top.astype(BF)
-        for place in range(nz):
-            @pl.when(z != place)
-            def _():
-                send(cz_send.at[c], cz_recv.at[c, flip(z, place)], 9 + c, {"sub": place * ny + y})
+        for k in range(nz - 1):
+            send(cz_send.at[c], cz_recv.at[c, z], 9 + c, {"sub": (k + later(z, k)) * ny + y})
+        cz_recv[c, z] = cz_send[c]
 
     spread(t_hbm, rt, 1)
     spread(b_hbm, bt, 3)
     send(h_send, h_recv, 2, y_peer(1))
     vz[...] = down(tz, ly, lz)
 
+    lift_out[...] = jnp.concatenate(split(dot(uv[...], tv[0])), axis=1)
+    loads["d"].wait()
+    near_part(0, 2)
     rt[0] = tv[1]
     rt[5] = tv[2]
     bt[0] = bv[1]
@@ -300,19 +294,17 @@
     local = jnp.concatenate(local, axis=1) + dot(wide(mid_far), vw[...])
 
     for c in range(CHUNKS):
-        wait_bytes(cz_recv.at[c, pl.ds(1, nz - 1)], recv_sem.at[9 + c])
-        top = tops[c]
-        for j in range(1, nz):
-            top = top + cz_recv[c, j].astype(F32)
+        wait_bytes(cz_recv.at[c, pl.ds(0, nz - 1)], recv_sem.at[9 + c])
+        top = functools.reduce(jnp.add, [cz_recv[c, place].astype(F32) for place in range(nz)])
         at = pl.ds(c * half, half)
         pair_far = (local[c * half:(c + 1) * half] + dot(wide(top), vg[...])).astype(BF)
         for r in range(4):
-            far_y_send[r, at, :] = pair_far[:, r * rank:(r + 1) * rank]
-        for place in early(ny, 1):
-            @pl.when(y != place)
-            def _():
-                send(far_y_send.at[lax.div(flip(y, place), 2), at], far_y.at[part(y, c)], 11 + c, {"sub": z * ny + place})
-        far_y[part(y, c), :] = far_y_send[0, at, :]
+            far_y_send[flip(pair, r), at, :] = pair_far[:, r * rank:(r + 1) * rank]
+        for k in range(ny - 1):
+            place = jnp.where(rank_y > k, order[k], order[k + 1])
+            mate = jnp.where(rank_y > k, order[k] // 2, order[k + 1] // 2)
+            send(far_y_send.at[mate, at], far_y.at[part(y, c)], 11 + c, {"sub": z * ny + place})
+        far_y[part(y, c), :] = pair_far[:, :rank]
 
     wait_bytes(h_recv, recv_sem.at[2])
     far = dot_nt(h_recv[...], bv[0]).astype(BF)

time: 36.8 us -> 37.2 us (1.011)
  the two profiles are of different devices: /device:TPU:16 before, /device:TPU:1 now
where the time goes in v5:
time: 37.2 us; the launch traced here: 36.8 us
  Pallas kernels  36.8 us (99%)
    pallas_call x1, Pallas kernels, body(): pl.pallas_call(functools.partial(kernel, (lz, lx)), out_shape=[jax.ShapeD...  35.5 us
    pallas_call x1, Pallas kernels, body(): pl.pallas_call(last_kernel, out_shape=jax.ShapeDtypeStruct((leaf, vecs),...  1.31 us

profile of v5, /device:TPU:1, one launch (start us, length us, event | category | flops | bytes accessed | tf_op | source)
XLA Modules:
  0.0 36.8 jit_solution(460277098004614874)
XLA Ops:
  0.0 35.5 %shard_map.55 = (f32[1024,512]{1,0:T(8,128)S(1)}, bf16[1024,256]{1,0:T(8,128)(2,1)S(1)}, bf16[512,128]{1,0:T(8,128)(2,1)S(1)}) custom-call(bf16[1024,512]{1,0:T(8,128)(2,1)} %bitcast.7, bf16[1024,1024]{1,0:T(8,128)(2,1)} %bitcast.6, bf16[1024,128]{1,0:T(8,128)(2,1)} %bitcast.10, bf16[9,128,128]{2,1,0:T(8,128)(2,1)} %bitcast.8, bf16[9,128,128]{2,1,0:T(8,128)(2,1)} %bitcast.9), custom_call_target="tpu_custom_call" | custom-call | tf_op jit(solution)/shard_map/pallas_call | solution.py:392
  35.5 1.3 %shard_map.56 = bf16[1024,512]{1,0:T(8,128)(2,1)} custom-call(f32[1024,512]{1,0:T(8,128)S(1)} %get-tuple-element.8.near, bf16[1024,256]{1,0:T(8,128)(2,1)S(1)} %get-tuple-element.9.lift, bf16[512,128]{1,0:T(8,128)(2,1)S(1)} %get-tuple-element.10.far), custom_call_target="tpu_custom_call" | custom-call | tf_op jit(solution)/shard_map/pallas_call | solution.py:406

commit v6 on v5

--- a/solution.py
+++ b/solution.py
@@ -35,6 +35,13 @@
     for bit in range(offset.bit_length()):
         if offset >> bit & 1:
             out = out + (1 << bit) - (2 << bit) * lax.rem(lax.div(index, 1 << bit), 2)
+    return out
+
+
+def xor(left, right, bits):
+    out = 0
+    for bit in range(bits):
+        out = out + (1 << bit) * lax.rem(lax.div(left, 1 << bit) + lax.div(right, 1 << bit), 2)
     return out
 
 
@@ -128,6 +135,9 @@
 
     order = sorted(range(ny), key=lambda place: min(place, ny - place))
     rank_y = sum(jnp.where(y == place, k, 0) for k, place in enumerate(order))
+    chips = sorted(range(1, nx // 2), key=lambda place: min(place, nx // 2 - place))
+    places = [1, 0] + [2 * chip + core for chip in chips for core in range(2)]
+    rank_x = sum(jnp.where(grp == place, k, 0) for k, place in enumerate(places))
     barrier = pltpu.get_barrier_semaphore()
 
     def greet(sem, peer):
@@ -210,9 +220,11 @@
         share = dot(mids[c], wx[...])
         for i in range(lx):
             x_send[c, i] = share[:, i * rank:(i + 1) * rank].astype(BF)
-        for j in (4, 5, 6, 7, 2, 3, 1):
-            if j < nx:
-                send(x_send.at[c, level_of(j)], x_recv.at[c, j], 7 + c, x_peer(j))
+        for k in range(nx - 1):
+            target = jnp.where(rank_x > k, places[k], places[k + 1])
+            apart = xor(grp, target, lx)
+            level = sum(jnp.where(apart >= 1 << i, 1, 0) for i in range(1, lx))
+            send(x_send.at[c, level], x_recv.at[c, apart], 7 + c, {"grp": target})
 
     mid_w = jnp.concatenate(mids, axis=0)
     zs_send[0] = mid_w[:, :rank]

time: 37.2 us -> 37.2 us (level)
  no operation moved by 1% of the time
where the time goes in v6:
time: 37.2 us; the launch traced here: 36.5 us
  Pallas kernels  36.5 us (98%)
    pallas_call x1, Pallas kernels, body(): pl.pallas_call(functools.partial(kernel, (lz, lx)), out_shape=[jax.ShapeD...  35.2 us
    pallas_call x1, Pallas kernels, body(): pl.pallas_call(last_kernel, out_shape=jax.ShapeDtypeStruct((leaf, vecs),...  1.31 us

profile of v6, /device:TPU:1, one launch (start us, length us, event | category | flops | bytes accessed | tf_op | source)
XLA Modules:
  0.0 36.5 jit_solution(2463953382794263248)
XLA Ops:
  0.0 35.2 %shard_map.55 = (f32[1024,512]{1,0:T(8,128)S(1)}, bf16[1024,256]{1,0:T(8,128)(2,1)S(1)}, bf16[512,128]{1,0:T(8,128)(2,1)S(1)}) custom-call(bf16[1024,512]{1,0:T(8,128)(2,1)} %bitcast.7, bf16[1024,1024]{1,0:T(8,128)(2,1)} %bitcast.6, bf16[1024,128]{1,0:T(8,128)(2,1)} %bitcast.10, bf16[9,128,128]{2,1,0:T(8,128)(2,1)} %bitcast.8, bf16[9,128,128]{2,1,0:T(8,128)(2,1)} %bitcast.9), custom_call_target="tpu_custom_call" | custom-call | tf_op jit(solution)/shard_map/pallas_call | solution.py:404
  35.2 1.3 %shard_map.56 = bf16[1024,512]{1,0:T(8,128)(2,1)} custom-call(f32[1024,512]{1,0:T(8,128)S(1)} %get-tuple-element.8.near, bf16[1024,256]{1,0:T(8,128)(2,1)S(1)} %get-tuple-element.9.lift, bf16[512,128]{1,0:T(8,128)(2,1)S(1)} %get-tuple-element.10.far), custom_call_target="tpu_custom_call" | custom-call | tf_op jit(solution)/shard_map/pallas_call | solution.py:418

commit v7 on v6

--- a/solution.py
+++ b/solution.py
@@ -204,6 +204,8 @@
         def _():
             greet(z_sem, {"sub": place * ny + y})
 
+    cl_send[...] = dot(hat_w[:, :2 * rank], jnp.concatenate([tv[0], tv[0]], axis=0)).astype(BF)
+    h_send[...] = hat.astype(BF)
     loads["t1"].wait()
     tz = climb(ly, lz + lx - 1)
     wx[...] = jnp.concatenate([up_weight(product) for product in tz[lz - 1:]], axis=1)
@@ -240,10 +242,11 @@
 
     for j in far_first(nz):
         send(zs_send.at[level_of(j)], zs_recv.at[j], 4, z_peer(j))
-    cl_send[...] = dot(hat_w[:, :2 * rank], jnp.concatenate([tv[0], tv[0]], axis=0)).astype(BF)
-    h_send[...] = hat.astype(BF)
     for j in far_first(ny):
         send(cl_send.at[rows(flip(y, j), yblk)], cl_recv.at[j], 0, y_peer(j))
+    spread(t_hbm, rt, 1)
+    spread(b_hbm, bt, 3)
+    send(h_send, h_recv, 2, y_peer(1))
 
     for c in range(CHUNKS):
         wait_bytes(x_recv.at[c, pl.ds(1, nx - 1)], recv_sem.at[7 + c])
@@ -256,9 +259,6 @@
             send(cz_send.at[c], cz_recv.at[c, z], 9 + c, {"sub": (k + later(z, k)) * ny + y})
         cz_recv[c, z] = cz_send[c]
 
-    spread(t_hbm, rt, 1)
-    spread(b_hbm, bt, 3)
-    send(h_send, h_recv, 2, y_peer(1))
     vz[...] = down(tz, ly, lz)
 
     lift_out[...] = jnp.concatenate(split(dot(uv[...], tv[0])), axis=1)

time: 37.2 us -> 37 us (level)
  the two profiles are of different devices: /device:TPU:1 before, /device:TPU:16 now
where the time goes in v7:
time: 37 us; the launch traced here: 36.8 us
  Pallas kernels  36.8 us (99%)
    pallas_call x1, Pallas kernels, body(): pl.pallas_call(functools.partial(kernel, (lz, lx)), out_shape=[jax.ShapeD...  35.5 us
    pallas_call x1, Pallas kernels, body(): pl.pallas_call(last_kernel, out_shape=jax.ShapeDtypeStruct((leaf, vecs),...  1.31 us

profile of v7, /device:TPU:16, one launch (start us, length us, event | category | flops | bytes accessed | tf_op | source)
XLA Modules:
  0.0 36.8 jit_solution(17816598639874342087)
XLA Ops:
  0.0 35.5 %shard_map.55 = (f32[1024,512]{1,0:T(8,128)S(1)}, bf16[1024,256]{1,0:T(8,128)(2,1)S(1)}, bf16[512,128]{1,0:T(8,128)(2,1)S(1)}) custom-call(bf16[1024,512]{1,0:T(8,128)(2,1)} %bitcast.7, bf16[1024,1024]{1,0:T(8,128)(2,1)} %bitcast.6, bf16[1024,128]{1,0:T(8,128)(2,1)} %bitcast.10, bf16[9,128,128]{2,1,0:T(8,128)(2,1)} %bitcast.8, bf16[9,128,128]{2,1,0:T(8,128)(2,1)} %bitcast.9), custom_call_target="tpu_custom_call" | custom-call | tf_op jit(solution)/shard_map/pallas_call | solution.py:404
  35.5 1.3 %shard_map.56 = bf16[1024,512]{1,0:T(8,128)(2,1)} custom-call(f32[1024,512]{1,0:T(8,128)S(1)} %get-tuple-element.8.near, bf16[1024,256]{1,0:T(8,128)(2,1)S(1)} %get-tuple-element.9.lift, bf16[512,128]{1,0:T(8,128)(2,1)S(1)} %get-tuple-element.10.far), custom_call_target="tpu_custom_call" | custom-call | tf_op jit(solution)/shard_map/pallas_call | solution.py:418

commit v8 on v7

--- a/solution.py
+++ b/solution.py
@@ -133,8 +133,7 @@
     for name in ("t", "u", "x0", "x1"):
         loads[name].start()
 
-    order = sorted(range(ny), key=lambda place: min(place, ny - place))
-    rank_y = sum(jnp.where(y == place, k, 0) for k, place in enumerate(order))
+    first = (grp == 1) & (y > 0)
     chips = sorted(range(1, nx // 2), key=lambda place: min(place, nx // 2 - place))
     places = [1, 0] + [2 * chip + core for chip in chips for core in range(2)]
     rank_x = sum(jnp.where(grp == place, k, 0) for k, place in enumerate(places))
@@ -312,10 +311,12 @@
         pair_far = (local[c * half:(c + 1) * half] + dot(wide(top), vg[...])).astype(BF)
         for r in range(4):
             far_y_send[flip(pair, r), at, :] = pair_far[:, r * rank:(r + 1) * rank]
-        for k in range(ny - 1):
-            place = jnp.where(rank_y > k, order[k], order[k + 1])
-            mate = jnp.where(rank_y > k, order[k] // 2, order[k + 1] // 2)
-            send(far_y_send.at[mate, at], far_y.at[part(y, c)], 11 + c, {"sub": z * ny + place})
+        apart = far_first(ny)
+        own = sum(jnp.where(y == j, k, 0) for k, j in enumerate(apart))
+        for k, j in enumerate(apart):
+            j = jnp.where(first, jnp.where(own >= k, apart[max(k - 1, 0)], j) if k else y, j)
+            place = xor(y, j, ly)
+            send(far_y_send.at[lax.div(place, 2), at], far_y.at[part(y, c)], 11 + c, {"sub": z * ny + place})
         far_y[part(y, c), :] = pair_far[:, :rank]
 
     wait_bytes(h_recv, recv_sem.at[2])

time: 37 us -> 36.6 us (0.989)
  the two profiles are of different devices: /device:TPU:16 before, /device:TPU:1 now
where the time goes in v8:
time: 36.6 us; the launch traced here: 36 us
  Pallas kernels  35.9 us (98%)
    pallas_call x1, Pallas kernels, body(): pl.pallas_call(functools.partial(kernel, (lz, lx)), out_shape=[jax.ShapeD...  34.6 us
    pallas_call x1, Pallas kernels, body(): pl.pallas_call(last_kernel, out_shape=jax.ShapeDtypeStruct((leaf, vecs),...  1.31 us

profile of v8, /device:TPU:1, one launch (start us, length us, event | category | flops | bytes accessed | tf_op | source)
XLA Modules:
  0.0 36.0 jit_solution(15343115149852798189)
XLA Ops:
  0.0 34.6 %shard_map.55 = (f32[1024,512]{1,0:T(8,128)S(1)}, bf16[1024,256]{1,0:T(8,128)(2,1)S(1)}, bf16[512,128]{1,0:T(8,128)(2,1)S(1)}) custom-call(bf16[1024,512]{1,0:T(8,128)(2,1)} %bitcast.7, bf16[1024,1024]{1,0:T(8,128)(2,1)} %bitcast.6, bf16[1024,128]{1,0:T(8,128)(2,1)} %bitcast.10, bf16[9,128,128]{2,1,0:T(8,128)(2,1)} %bitcast.8, bf16[9,128,128]{2,1,0:T(8,128)(2,1)} %bitcast.9), custom_call_target="tpu_custom_call" | custom-call | tf_op jit(solution)/shard_map/pallas_call | solution.py:405
  34.7 1.3 %shard_map.56 = bf16[1024,512]{1,0:T(8,128)(2,1)} custom-call(f32[1024,512]{1,0:T(8,128)S(1)} %get-tuple-element.8.near, bf16[1024,256]{1,0:T(8,128)(2,1)S(1)} %get-tuple-element.9.lift, bf16[512,128]{1,0:T(8,128)(2,1)S(1)} %get-tuple-element.10.far), custom_call_target="tpu_custom_call" | custom-call | tf_op jit(solution)/shard_map/pallas_call | solution.py:419

commit v9 on v2

--- a/solution.py
+++ b/solution.py
@@ -46,7 +46,7 @@
 
 
 def early(count, cores):
-    ring = sorted(range(count), key=lambda place: min(place, count - place))
+    ring = sorted(range(count), key=lambda place: place if place < count // 2 else count - place + 1.5)
     return [place * cores + core for place in ring for core in reversed(range(cores))]
 
 
@@ -66,6 +66,14 @@
 def wide(value):
     high, low = split(value)
     return jnp.concatenate([high, low, high], axis=1)
+
+
+def twice(product):
+    return jnp.concatenate([product.astype(BF)] * 2, axis=0)
+
+
+def tight(value):
+    return jnp.concatenate(split(value), axis=1)
 
 
 def times_exact(product, matrix):
@@ -153,10 +161,10 @@
             chain.append(product)
         return chain
 
-    def down(products, base, levels):
+    def down(products, base, levels, rows_of):
         parts = [bv[base].T]
         for i in range(1, levels):
-            parts.append(up_weight(times_exact(products[i - 1], bv[base + i]).T))
+            parts.append(rows_of(times_exact(products[i - 1], bv[base + i]).T))
         return jnp.concatenate(parts, axis=0)
 
     def near_part(part, parts):
@@ -186,21 +194,21 @@
     cl_send[...] = dot(hat_w[:, :2 * rank], jnp.concatenate([tv[0], tv[0]], axis=0)).astype(BF)
     h_send[...] = hat.astype(BF)
     tz = climb(ly, lz + lx - 1)
-    wx[...] = jnp.concatenate([up_weight(product) for product in tz[lz - 1:]], axis=1)
+    wx[...] = jnp.concatenate([twice(product) for product in tz[lz - 1:]], axis=1)
     if lz > 1:
         wzl[...] = jnp.concatenate([up_exact(tv[ly])] + [up_weight(tz[i]) for i in range(1, lz - 1)], axis=1)
     lift_out[...] = jnp.concatenate(split(dot(uv[...], tv[0])), axis=1)
     loads["d"].wait()
     near_part(0, 2)
     loads["b"].wait()
-    vx[...] = down(climb(ly + lz, lx), ly + lz, lx)
+    vx[...] = down(climb(ly + lz, lx), ly + lz, lx, twice)
 
     wait_bytes(cy_recv.at[pl.ds(1, ny - 1)], recv_sem.at[0])
     mid = cy_send[rows(y, yblk), :].astype(F32)
     for j in range(1, ny):
         mid = mid + cy_recv[j].astype(F32)
     mid_w = wide(mid)
-    share = dot(mid_w, wx[...])
+    share = dot(mid_w[:, :2 * rank], wx[...])
     for i in range(lx):
         x_send[i] = share[:, i * rank:(i + 1) * rank].astype(BF)
     for place in early(nx // 2, 2):
@@ -230,7 +238,7 @@
     wait_bytes(x_recv.at[pl.ds(1, nx - 1)], recv_sem.at[6])
     parts = [x_recv[1]]
     for level in range(1, lx):
-        parts.append(wide(functools.reduce(jnp.add, [x_recv[j].astype(F32) for j in range(1 << level, 2 << level)])))
+        parts.append(tight(functools.reduce(jnp.add, [x_recv[j].astype(F32) for j in range(1 << level, 2 << level)])))
     top = dot(jnp.concatenate(parts, axis=1), vx[...])
     cz_send[...] = top.astype(BF)
     for place in range(nz):
@@ -238,7 +246,7 @@
         def _():
             send(cz_send, cz_recv.at[flip(z, place)], 3, {"sub": place * ny + y})
 
-    vz[...] = down(tz, ly, lz)
+    vz[...] = down(tz, ly, lz, up_weight)
 
     rt[0] = tv[1]
     rt[5] = tv[2]
@@ -250,11 +258,11 @@
         both = jnp.concatenate([rt[2 * quad], rt[2 * quad + 1]], axis=0)
         lifts.append(dot(both, rt[5 - quad]))
     lifts = jnp.concatenate(lifts, axis=0)
-    whole = dot(wide(lifts), wx[:, :rank])
+    whole = dot(wide(lifts), up_weight(tz[lz - 1]))
     for r in range(4):
         at = slice(r * rank, (r + 1) * rank)
         vw[:, at] = up_weight(lifts[at].T)
-        vg[:, at] = up_weight(whole[at].T)
+        vg[:, at] = twice(whole[at].T)
     wait_bytes(zs_recv.at[pl.ds(1, nz - 1)], recv_sem.at[4])
     parts = [zs_recv[1]]
     for level in range(1, lz):
@@ -284,7 +292,7 @@
     wait_bytes(cz_recv.at[pl.ds(1, nz - 1)], recv_sem.at[3])
     for j in range(1, nz):
         top = top + cz_recv[j].astype(F32)
-    pair_far = (local + dot(wide(top), vg[...])).astype(BF)
+    pair_far = (local + dot(tight(top), vg[...])).astype(BF)
     for r in range(4):
         far_y_send[r] = pair_far[:, r * rank:(r + 1) * rank]
     for place in early(ny, 1):
@@ -348,12 +356,12 @@
             pltpu.VMEM((6, rank, rank), BF),
             pltpu.VMEM((6, rank, rank), BF),
             pltpu.VMEM((3 * rank, rank), BF),
-            pltpu.VMEM((3 * rank, lx * rank), BF),
+            pltpu.VMEM((2 * rank, lx * rank), BF),
             pltpu.VMEM((3 * rank, max(1, lz - 1) * rank), BF),
-            pltpu.VMEM(((3 * lx - 2) * rank, rank), BF),
+            pltpu.VMEM(((2 * lx - 1) * rank, rank), BF),
             pltpu.VMEM(((3 * lz - 2) * rank, rank), BF),
             pltpu.VMEM((3 * rank, 4 * rank), BF),
-            pltpu.VMEM((3 * rank, 4 * rank), BF),
+            pltpu.VMEM((2 * rank, 4 * rank), BF),
             pltpu.VMEM((vecs, rank), BF),
             pltpu.VMEM((vecs, rank), BF),
             pltpu.VMEM((vecs, rank), BF),

time: 36.3 us -> 36.1 us (level)
  no operation moved by 1% of the time
where the time goes in v9:
time: 36.1 us; the launch traced here: 35.8 us
  Pallas kernels  35.8 us (99%)
    pallas_call x1, Pallas kernels, body(): pl.pallas_call(functools.partial(kernel, (lz, lx)), out_shape=[jax.ShapeD...  34.5 us
    pallas_call x1, Pallas kernels, body(): pl.pallas_call(last_kernel, out_shape=jax.ShapeDtypeStruct((leaf, vecs),...  1.31 us

profile of v9, /device:TPU:1, one launch (start us, length us, event | category | flops | bytes accessed | tf_op | source)
XLA Modules:
  0.0 35.8 jit_solution(9085693115052318723)
XLA Ops:
  0.0 34.5 %shard_map.55 = (f32[1024,512]{1,0:T(8,128)S(1)}, bf16[1024,256]{1,0:T(8,128)(2,1)S(1)}, bf16[512,128]{1,0:T(8,128)(2,1)S(1)}) custom-call(bf16[1024,512]{1,0:T(8,128)(2,1)} %bitcast.7, bf16[1024,1024]{1,0:T(8,128)(2,1)} %bitcast.6, bf16[1024,128]{1,0:T(8,128)(2,1)} %bitcast.10, bf16[9,128,128]{2,1,0:T(8,128)(2,1)} %bitcast.8, bf16[9,128,128]{2,1,0:T(8,128)(2,1)} %bitcast.9), custom_call_target="tpu_custom_call" | custom-call | tf_op jit(solution)/shard_map/pallas_call | solution.py:385
  34.5 1.3 %shard_map.56 = bf16[1024,512]{1,0:T(8,128)(2,1)} custom-call(f32[1024,512]{1,0:T(8,128)S(1)} %get-tuple-element.8.near, bf16[1024,256]{1,0:T(8,128)(2,1)S(1)} %get-tuple-element.9.lift, bf16[512,128]{1,0:T(8,128)(2,1)S(1)} %get-tuple-element.10.far), custom_call_target="tpu_custom_call" | custom-call | tf_op jit(solution)/shard_map/pallas_call | solution.py:399

commit v10 on v2

--- a/solution.py
+++ b/solution.py
@@ -46,7 +46,7 @@
 
 
 def early(count, cores):
-    ring = sorted(range(count), key=lambda place: min(place, count - place))
+    ring = sorted(range(count), key=lambda place: place if place < count // 2 else count - place + 1.5)
     return [place * cores + core for place in ring for core in reversed(range(cores))]
 
 

time: 36.3 us -> 36.2 us (level)
  no operation moved by 1% of the time
where the time goes in v10:
time: 36.2 us; the launch traced here: 35.9 us
  Pallas kernels  35.9 us (99%)
    pallas_call x1, Pallas kernels, body(): pl.pallas_call(functools.partial(kernel, (lz, lx)), out_shape=[jax.ShapeD...  34.6 us
    pallas_call x1, Pallas kernels, body(): pl.pallas_call(last_kernel, out_shape=jax.ShapeDtypeStruct((leaf, vecs),...  1.31 us

profile of v10, /device:TPU:1, one launch (start us, length us, event | category | flops | bytes accessed | tf_op | source)
XLA Modules:
  0.0 35.9 jit_solution(12367832925027284547)
XLA Ops:
  0.0 34.6 %shard_map.55 = (f32[1024,512]{1,0:T(8,128)S(1)}, bf16[1024,256]{1,0:T(8,128)(2,1)S(1)}, bf16[512,128]{1,0:T(8,128)(2,1)S(1)}) custom-call(bf16[1024,512]{1,0:T(8,128)(2,1)} %bitcast.7, bf16[1024,1024]{1,0:T(8,128)(2,1)} %bitcast.6, bf16[1024,128]{1,0:T(8,128)(2,1)} %bitcast.10, bf16[9,128,128]{2,1,0:T(8,128)(2,1)} %bitcast.8, bf16[9,128,128]{2,1,0:T(8,128)(2,1)} %bitcast.9), custom_call_target="tpu_custom_call" | custom-call | tf_op jit(solution)/shard_map/pallas_call | solution.py:377
  34.6 1.3 %shard_map.56 = bf16[1024,512]{1,0:T(8,128)(2,1)} custom-call(f32[1024,512]{1,0:T(8,128)S(1)} %get-tuple-element.8.near, bf16[1024,256]{1,0:T(8,128)(2,1)S(1)} %get-tuple-element.9.lift, bf16[512,128]{1,0:T(8,128)(2,1)S(1)} %get-tuple-element.10.far), custom_call_target="tpu_custom_call" | custom-call | tf_op jit(solution)/shard_map/pallas_call | solution.py:391

commit v11 on v10

--- a/solution.py
+++ b/solution.py
@@ -132,7 +132,8 @@
         ("b", b_hbm, bv),
     )):
         loads[name] = pltpu.make_async_copy(src, dst, load_sem.at[i])
-        loads[name].start()
+        if name not in ("b", "d"):
+            loads[name].start()
 
     pair = lax.div(y, 2)
     outward = 2 * lax.rem(y, 2) - 1
@@ -172,16 +173,18 @@
     loads["x0"].wait()
     hat_t = dot(ut[:, :head], xv[:head, :])
     loads["x1"].wait()
+    loads["b"].start()
+    loads["d"].start()
     hat = (hat_t + dot(ut[:, head:], xv[head:, :])).T
     hat_w = wide(hat)
     cy_send[...] = dot(hat_w, wy[...]).astype(BF)
     pl.semaphore_wait(barrier, ny - 1 + nx - 1 + z)
+    for j in far_first(ny):
+        send(cy_send.at[rows(flip(y, j), yblk)], cy_recv.at[j], 0, y_peer(j))
     for place in range(nz):
         @pl.when(z > place)
         def _():
             greet(z_sem, {"sub": place * ny + y})
-    for j in far_first(ny):
-        send(cy_send.at[rows(flip(y, j), yblk)], cy_recv.at[j], 0, y_peer(j))
 
     cl_send[...] = dot(hat_w[:, :2 * rank], jnp.concatenate([tv[0], tv[0]], axis=0)).astype(BF)
     h_send[...] = hat.astype(BF)

time: 36.2 us -> 36.2 us (level)
  no operation moved by 1% of the time
where the time goes in v11:
time: 36.2 us; the launch traced here: 35.9 us
  Pallas kernels  35.9 us (99%)
    pallas_call x1, Pallas kernels, body(): pl.pallas_call(functools.partial(kernel, (lz, lx)), out_shape=[jax.ShapeD...  34.6 us
    pallas_call x1, Pallas kernels, body(): pl.pallas_call(last_kernel, out_shape=jax.ShapeDtypeStruct((leaf, vecs),...  1.31 us

profile of v11, /device:TPU:1, one launch (start us, length us, event | category | flops | bytes accessed | tf_op | source)
XLA Modules:
  0.0 35.9 jit_solution(10735413756608991875)
XLA Ops:
  0.0 34.6 %shard_map.55 = (f32[1024,512]{1,0:T(8,128)S(1)}, bf16[1024,256]{1,0:T(8,128)(2,1)S(1)}, bf16[512,128]{1,0:T(8,128)(2,1)S(1)}) custom-call(bf16[1024,512]{1,0:T(8,128)(2,1)} %bitcast.7, bf16[1024,1024]{1,0:T(8,128)(2,1)} %bitcast.6, bf16[1024,128]{1,0:T(8,128)(2,1)} %bitcast.10, bf16[9,128,128]{2,1,0:T(8,128)(2,1)} %bitcast.8, bf16[9,128,128]{2,1,0:T(8,128)(2,1)} %bitcast.9), custom_call_target="tpu_custom_call" | custom-call | tf_op jit(solution)/shard_map/pallas_call | solution.py:380
  34.6 1.3 %shard_map.56 = bf16[1024,512]{1,0:T(8,128)(2,1)} custom-call(f32[1024,512]{1,0:T(8,128)S(1)} %get-tuple-element.8.near, bf16[1024,256]{1,0:T(8,128)(2,1)S(1)} %get-tuple-element.9.lift, bf16[512,128]{1,0:T(8,128)(2,1)S(1)} %get-tuple-element.10.far), custom_call_target="tpu_custom_call" | custom-call | tf_op jit(solution)/shard_map/pallas_call | solution.py:394
